TPU v7x, 32 devices: a whole 2x2x4 slice. The times are simulated.
32 devices in a mesh: dp: 8 (over z, x), section: 4 (over y, core).
Axes of the slice: x: 2, y: 2, z: 4, core: 2. Of those that a mesh axis runs over, the one named last changes fastest.
Arguments:
- images_in: bfloat16 [2048, 4096], P(('dp', 'section')), may hold values from -6 to 6
- labels: int32 [2048], P(('dp', 'section')), may hold values from 0 to 9
- conv_weight: float32 [3, 2, 576, 64], P(None, None, None, 'section'), may hold values from -0.25 to 0.25
- frn_gain: float32 [3, 2, 64], replicated, may hold values from 0.25 to 1.75
- frn_bias: float32 [3, 2, 64], replicated, may hold values from -3 to 3
- head_weight: float32 [64, 10], replicated, as said below
- head_bias: float32 [10], replicated, may hold values from -4 to 4
Outputs:
- grad_conv: float32 [3, 2, 576, 64], P(None, None, None, 'section')
- grad_norm: float32 [3, 2, 2, 64], replicated
- grad_head_weight: float32 [64, 10], replicated
- grad_head_bias: float32 [10], replicated
Inputs may be any that keep to these rules, and one draw needn't show every extreme that they name: `head_weight`: the classifier's weights.
All inputs are finite; a program needn't handle non-finite values.
Results may differ from a plain program's by a relative error of at most 0.0033.
The roundings to bfloat16 on the way count: a program that leaves them out, or rounds other values in their place, can miss the bound.
Values may be sent and summed in bfloat16 or wider, within the bound.
A program may use at most 64 MiB of HBM per device.

v0:
```python
import jax
import jax.numpy as jnp
from jax import lax
from jax.sharding import PartitionSpec as P

SIDE = 8
MICRO = 8
eps = 1e-06
prior_precision = 0.5


def make_patches(maps):
    side = maps.shape[1]
    padded = jnp.pad(maps, ((0, 0), (1, 1), (1, 1), (0, 0)))
    taps = [padded[:, a : a + side, e : e + side, :] for a in range(3) for e in range(3)]
    stacked = jnp.concatenate(taps, axis=3)
    return stacked.reshape(maps.shape[0] * side * side, 9 * maps.shape[3])


def fold_patches(columns, shape):
    back = jax.vjp(make_patches, jnp.zeros(shape, jnp.float32))[1]
    return back(columns)[0]


def respond(values, gain, bias, count):
    grouped = values.reshape(count, -1, values.shape[1])
    energy = jnp.mean(grouped * grouped, axis=1, keepdims=True)
    normed = grouped * lax.rsqrt(energy + eps)
    return (gain * normed + bias).reshape(values.shape)


def swish(values):
    return values * jax.nn.sigmoid(values)


def block_forward(maps, weights, gains, biases):
    count = maps.shape[0]
    w_first = weights[0]
    w_second = weights[1]
    cols_first = make_patches(maps)
    pre_first = jnp.dot(cols_first, w_first, preferred_element_type=jnp.float32)
    hidden = swish(respond(pre_first, gains[0], biases[0], count)).astype(jnp.bfloat16)
    cols_second = make_patches(hidden.reshape(maps.shape))
    pre_second = jnp.dot(cols_second, w_second, preferred_element_type=jnp.float32)
    skip = maps.reshape(pre_second.shape).astype(jnp.float32)
    result = swish(skip + respond(pre_second, gains[1], biases[1], count)).astype(jnp.bfloat16)
    return (result.reshape(maps.shape), (cols_first, pre_first, cols_second, pre_second))


def block_backward(maps, cotangent, weights, gains, biases):
    count = maps.shape[0]
    w_first = weights[0]
    w_second = weights[1]
    saved = block_forward(maps, weights, gains, biases)[1]
    cols_first, pre_first, cols_second, pre_second = saved

    def second_part(values, skip, gain, bias):
        return swish(skip + respond(values, gain, bias, count))

    def first_part(values, gain, bias):
        return swish(respond(values, gain, bias, count))

    skip = maps.reshape(pre_second.shape).astype(jnp.float32)
    back_second = jax.vjp(second_part, pre_second, skip, gains[1], biases[1])[1]
    d_second, d_skip, dg_second, db_second = back_second(
        cotangent.reshape(pre_second.shape).astype(jnp.float32)
    )
    q_second = d_second.astype(jnp.bfloat16)
    dw_second = jnp.dot(cols_second.T, q_second, preferred_element_type=jnp.float32)
    d_hidden = fold_patches(
        jnp.dot(q_second, w_second.T, preferred_element_type=jnp.float32), maps.shape
    )
    back_first = jax.vjp(first_part, pre_first, gains[0], biases[0])[1]
    d_first, dg_first, db_first = back_first(d_hidden.reshape(pre_first.shape))
    q_first = d_first.astype(jnp.bfloat16)
    dw_first = jnp.dot(cols_first.T, q_first, preferred_element_type=jnp.float32)
    d_input = fold_patches(
        jnp.dot(q_first, w_first.T, preferred_element_type=jnp.float32), maps.shape
    )
    d_maps = (d_skip.reshape(maps.shape) + d_input).astype(jnp.bfloat16)
    d_norm = jnp.stack([jnp.stack([dg_first, db_first]), jnp.stack([dg_second, db_second])])
    return (d_maps, jnp.stack([dw_first, dw_second]), d_norm)


def head_grads(final, labels, head_w, head_b, total):
    count = final.shape[0]
    width = final.shape[3]
    pixels = final.shape[1] * final.shape[2]
    pooled = jnp.mean(final.reshape(count, pixels, width).astype(jnp.float32), axis=1)
    logits = jnp.dot(pooled, head_w, precision=lax.Precision.HIGHEST) + head_b
    top = jnp.max(logits, axis=1, keepdims=True)
    expo = jnp.exp(logits - top)
    probs = expo / jnp.sum(expo, axis=1, keepdims=True)
    onehot = (labels[:, None] == jnp.arange(head_w.shape[1])[None, :]).astype(jnp.float32)
    d_logits = (probs - onehot) / total
    d_head_w = jnp.dot(pooled.T, d_logits, precision=lax.Precision.HIGHEST)
    d_head_b = jnp.sum(d_logits, axis=0)
    d_pooled = jnp.dot(d_logits, head_w.T, precision=lax.Precision.HIGHEST) / pixels
    spread = jnp.broadcast_to(d_pooled[:, None, :], (count, pixels, width))
    return (spread.astype(jnp.bfloat16).reshape(final.shape), d_head_w, d_head_b)


def group_grads(maps, labels, weights, gains, biases, head_w, head_b, total):
    saved = []
    for index in range(weights.shape[0]):
        saved.append(maps)
        maps = block_forward(maps, weights[index], gains[index], biases[index])[0]
    cotangent, d_head_w, d_head_b = head_grads(maps, labels, head_w, head_b, total)
    conv_terms = []
    norm_terms = []
    for index in reversed(range(weights.shape[0])):
        cotangent, d_conv, d_norm = block_backward(
            saved[index], cotangent, weights[index], gains[index], biases[index]
        )
        conv_terms.insert(0, d_conv)
        norm_terms.insert(0, d_norm)
    return (jnp.stack(conv_terms), jnp.stack(norm_terms), d_head_w, d_head_b)


def accumulate(maps, labels, weights, gains, biases, head_w, head_b, total):
    width = weights.shape[3]
    initial = (
        jnp.zeros(weights.shape, jnp.float32),
        jnp.zeros((weights.shape[0], 2, 2, width), jnp.float32),
        jnp.zeros(head_w.shape, jnp.float32),
        jnp.zeros(head_b.shape, jnp.float32),
    )

    def advance(carry, item):
        terms = group_grads(item[0], item[1], weights, gains, biases, head_w, head_b, total)
        return (tuple((left + right for left, right in zip(carry, terms))), None)

    return lax.scan(advance, initial, (maps, labels))[0]


def per_device(images_in, labels, conv_weight, frn_gain, frn_bias, head_weight, head_bias):
    images = images_in.shape[0]
    width = frn_gain.shape[2]
    share = conv_weight.shape[3]
    total = images * lax.axis_size("dp") * lax.axis_size("section")
    offset = lax.axis_index("section") * share
    rounded_share = conv_weight.astype(jnp.bfloat16)
    all_conv = lax.all_gather(rounded_share, "section", axis=3, tiled=True)
    group_size = images // MICRO
    maps = images_in.reshape(MICRO, group_size, SIDE, SIDE, width)
    label_groups = labels.reshape(MICRO, group_size)
    conv_grad, norm_grad, head_w_grad, head_b_grad = accumulate(
        maps, label_groups, all_conv, frn_gain, frn_bias, head_weight, head_bias, total
    )
    summed = lax.psum(conv_grad, ("dp", "section"))
    conv_owned = lax.dynamic_slice_in_dim(summed, offset, share, 3)
    norm_sum, head_w_sum, head_b_sum = lax.psum(
        (norm_grad, head_w_grad, head_b_grad), ("dp", "section")
    )
    params = jnp.stack([frn_gain, frn_bias], axis=2)
    return (
        conv_owned + prior_precision * conv_weight,
        norm_sum + prior_precision * params,
        head_w_sum + prior_precision * head_weight,
        head_b_sum + prior_precision * head_bias,
    )


def solution(mesh):
    return jax.shard_map(
        per_device,
        mesh=mesh,
        in_specs=(
            P(("dp", "section"), None),
            P(("dp", "section")),
            P(None, None, None, "section"),
            P(),
            P(),
            P(),
            P(),
        ),
        out_specs=(P(None, None, None, "section"), P(), P(), P()),
        check_vma=False,
    )
```

profile of v0, /device:TPU:0, one launch (start us, length us, event | category | flops | bytes accessed | tf_op | source)
XLA Modules:
  0.0 816.5 jit_solution(12413973247500979296)
XLA Ops:
  9.6 8.5 %all_gather.3 = bf16[3,2,576,64]{2,3,1,0:T(8,128)(2,1)S(1)} all-gather(bf16[3,2,576,16]{2,3,1,0:T(8,128)(2,1)S(1)} %convert_element_type.386), channel_id=1, replica_groups=mesh['dp'=8,'section'=4] {'section'}, dimensions={3}, use_global_device_ids=true | all-gather | bytes 552960 | tf_op jit(solution)/shard_map/all_gather | solution.py:143
  19.2 659.0 %while.19 = (s32[]{:T(128)}, f32[3,2,576,64]{2,3,1,0:T(8,128)}, f32[3,2,2,64]{3,2,1,0:T(2,128)}, f32[64,10]{0,1:T(8,128)}, f32[10]{0:T(128)}, /*index=5*/bf16[8,...) while((s32[]{:T(128)}, f32[3,2,576,64]{2,3,1,0:T(8,128)}, ...), condition=%wide.region_29.30_spmd.clone, body=%wide.region_0.29_spmd.clone.sunk | while | flops 655682368 | bytes 99941760 | solution.py:133
  27.5 3.8 pad_slice_fusion.54
  37.1 4.0 pad_slice_fusion.55
  56.0 4.0 pad_slice_fusion.57
  69.6 4.0 fusion.302
  73.6 2.2 concatenate.404
  109.9 3.8 pad_slice_fusion.54
  119.4 4.0 pad_slice_fusion.55
  138.3 4.0 pad_slice_fusion.57
  152.0 4.0 fusion.302
  156.0 2.2 concatenate.404
  158.2 2.2 concatenate.405
  192.2 3.8 pad_slice_fusion.54
  201.8 4.0 pad_slice_fusion.55
  220.7 4.0 pad_slice_fusion.57
  234.3 4.0 fusion.302
  238.3 2.2 concatenate.404
  274.6 3.8 pad_slice_fusion.54
  284.2 4.0 pad_slice_fusion.55
  303.1 4.0 pad_slice_fusion.57
  316.7 4.0 fusion.302
  320.7 2.2 concatenate.404
  356.9 3.8 pad_slice_fusion.54
  366.5 4.0 pad_slice_fusion.55
  385.4 4.0 pad_slice_fusion.57
  399.1 4.0 fusion.302
  403.1 2.2 concatenate.404
  405.3 2.2 concatenate.405
  439.3 3.8 pad_slice_fusion.54
  448.9 4.0 pad_slice_fusion.55
  467.8 4.0 pad_slice_fusion.57
  481.4 4.0 fusion.302
  485.4 2.2 concatenate.404
  487.6 2.2 concatenate.405
  521.7 3.8 pad_slice_fusion.54
  531.3 4.0 pad_slice_fusion.55
  550.2 4.0 pad_slice_fusion.57
  563.8 4.0 fusion.302
  567.8 2.2 concatenate.404
  570.0 2.2 concatenate.405
  604.0 3.8 pad_slice_fusion.54
  613.6 4.0 pad_slice_fusion.55
  632.5 4.0 pad_slice_fusion.57
  646.1 4.0 fusion.302
  650.2 2.2 concatenate.404
  678.2 40.8 %all-reduce.51 = (f32[3,2,2,64]{3,2,1,0:T(2,128)S(1)}, f32[64,10]{0,1:T(8,128)S(1)}, f32[10]{0:T(128)S(1)}) all-reduce(f32[3,2,2,64]{3,2,1,0:T(2,128)} %get-tuple-element.157, f32[64,10]{0,1:T(8,128)} %get-tuple-element.158, f32[10]{0:T(128)} %get-tuple-element.159), channel_id=1, replica_groups=mesh['dp'=8,'section'=4] {'dp','section'}, use_global_device_ids=true, to_apply=%region_31.32 | all-reduce | flops 1418 | bytes 11344 | tf_op jit(solution)/shard_map/psum | solution.py:152
  722.8 85.1 %all-reduce.54.cloned.1.call-done = f32[3,2,576,64]{2,3,1,0:T(8,128)} async-done(((f32[3,2,576,64]{2,3,1,0:T(8,128)}), f32[3,2,576,64]{2,3,1,0:T(8,128)}) %all-reduce.54.cloned.1.call-update) | async-done | bytes 884752 | tf_op jit(solution)/shard_map/psum | solution.py:150
  (1643 shorter events, 508.5 us)
Async XLA Ops:
  7.2 10.9 %copy-start.31 = (bf16[64,4096]{1,0:T(8,128)(2,1)S(1)}, bf16[64,4096]{1,0:T(8,128)(2,1)}, u32[]{:S(2)}) copy-start(bf16[64,4096]{1,0:T(8,128)(2,1)} %param.9) | copy-start | bytes 1572868
  7.2 800.7 %all-reduce.54.cloned.1.call-start = ((), (), s32[]{:S(2)}) async-start(), calls=%async_computation | async-start | bytes 1966080 | tf_op jit(solution)/shard_map/psum | solution.py:150
  19.2 4.6 copy-start.7
  19.2 23.2 %copy-start.5 = (bf16[3,2,576,64]{2,3,1,0:T(8,128)(2,1)}, bf16[3,2,576,64]{2,3,1,0:T(8,128)(2,1)S(1)}, u32[]{:S(2)}) copy-start(bf16[3,2,576,64]{2,3,1,0:T(8,128)(2,1)S(1)} %get-tuple-element.949) | copy-start | bytes 1327108 | tf_op jit(solution)/shard_map/while
  21.9 11.3 %copy-start.43 = (f32[64]{0:T(128)}, f32[64]{0:T(128)S(1)}, u32[]{:S(2)}) copy-start(f32[64]{0:T(128)S(1)} %get-tuple-element.737) | copy-start | bytes 772 | tf_op jit(solution)/shard_map/while
  21.9 20.9 %copy-start.40 = (f32[64]{0:T(128)}, f32[64]{0:T(128)S(1)}, u32[]{:S(2)}) copy-start(f32[64]{0:T(128)S(1)} %get-tuple-element.752) | copy-start | bytes 772 | tf_op jit(solution)/shard_map/while
  21.9 5.1 copy-start.11
  101.6 4.6 copy-start.7
  101.6 23.1 %copy-start.5 = (bf16[3,2,576,64]{2,3,1,0:T(8,128)(2,1)}, bf16[3,2,576,64]{2,3,1,0:T(8,128)(2,1)S(1)}, u32[]{:S(2)}) copy-start(bf16[3,2,576,64]{2,3,1,0:T(8,128)(2,1)S(1)} %get-tuple-element.949) | copy-start | bytes 1327108 | tf_op jit(solution)/shard_map/while
  104.2 11.3 %copy-start.43 = (f32[64]{0:T(128)}, f32[64]{0:T(128)S(1)}, u32[]{:S(2)}) copy-start(f32[64]{0:T(128)S(1)} %get-tuple-element.737) | copy-start | bytes 772 | tf_op jit(solution)/shard_map/while
  104.2 20.9 %copy-start.40 = (f32[64]{0:T(128)}, f32[64]{0:T(128)S(1)}, u32[]{:S(2)}) copy-start(f32[64]{0:T(128)S(1)} %get-tuple-element.752) | copy-start | bytes 772 | tf_op jit(solution)/shard_map/while
  104.3 5.1 copy-start.11
  128.8 4.3 copy-start.12
  184.0 4.6 copy-start.7
  184.0 23.1 %copy-start.5 = (bf16[3,2,576,64]{2,3,1,0:T(8,128)(2,1)}, bf16[3,2,576,64]{2,3,1,0:T(8,128)(2,1)S(1)}, u32[]{:S(2)}) copy-start(bf16[3,2,576,64]{2,3,1,0:T(8,128)(2,1)S(1)} %get-tuple-element.949) | copy-start | bytes 1327108 | tf_op jit(solution)/shard_map/while
  186.6 11.3 %copy-start.43 = (f32[64]{0:T(128)}, f32[64]{0:T(128)S(1)}, u32[]{:S(2)}) copy-start(f32[64]{0:T(128)S(1)} %get-tuple-element.737) | copy-start | bytes 772 | tf_op jit(solution)/shard_map/while
  186.6 20.9 %copy-start.40 = (f32[64]{0:T(128)}, f32[64]{0:T(128)S(1)}, u32[]{:S(2)}) copy-start(f32[64]{0:T(128)S(1)} %get-tuple-element.752) | copy-start | bytes 772 | tf_op jit(solution)/shard_map/while
  186.6 5.1 copy-start.11
  211.2 4.3 copy-start.12
  266.3 4.6 copy-start.7
  266.3 23.1 %copy-start.5 = (bf16[3,2,576,64]{2,3,1,0:T(8,128)(2,1)}, bf16[3,2,576,64]{2,3,1,0:T(8,128)(2,1)S(1)}, u32[]{:S(2)}) copy-start(bf16[3,2,576,64]{2,3,1,0:T(8,128)(2,1)S(1)} %get-tuple-element.949) | copy-start | bytes 1327108 | tf_op jit(solution)/shard_map/while
  268.9 11.3 %copy-start.43 = (f32[64]{0:T(128)}, f32[64]{0:T(128)S(1)}, u32[]{:S(2)}) copy-start(f32[64]{0:T(128)S(1)} %get-tuple-element.737) | copy-start | bytes 772 | tf_op jit(solution)/shard_map/while
  269.0 20.9 %copy-start.40 = (f32[64]{0:T(128)}, f32[64]{0:T(128)S(1)}, u32[]{:S(2)}) copy-start(f32[64]{0:T(128)S(1)} %get-tuple-element.752) | copy-start | bytes 772 | tf_op jit(solution)/shard_map/while
  269.0 5.1 copy-start.11
  293.5 4.3 copy-start.12
  348.7 4.6 copy-start.7
  348.7 23.1 %copy-start.5 = (bf16[3,2,576,64]{2,3,1,0:T(8,128)(2,1)}, bf16[3,2,576,64]{2,3,1,0:T(8,128)(2,1)S(1)}, u32[]{:S(2)}) copy-start(bf16[3,2,576,64]{2,3,1,0:T(8,128)(2,1)S(1)} %get-tuple-element.949) | copy-start | bytes 1327108 | tf_op jit(solution)/shard_map/while
  351.3 11.3 %copy-start.43 = (f32[64]{0:T(128)}, f32[64]{0:T(128)S(1)}, u32[]{:S(2)}) copy-start(f32[64]{0:T(128)S(1)} %get-tuple-element.737) | copy-start | bytes 772 | tf_op jit(solution)/shard_map/while
  351.3 20.9 %copy-start.40 = (f32[64]{0:T(128)}, f32[64]{0:T(128)S(1)}, u32[]{:S(2)}) copy-start(f32[64]{0:T(128)S(1)} %get-tuple-element.752) | copy-start | bytes 772 | tf_op jit(solution)/shard_map/while
  351.4 5.1 copy-start.11
  375.9 4.3 copy-start.12
  431.1 4.6 copy-start.7
  431.1 23.1 %copy-start.5 = (bf16[3,2,576,64]{2,3,1,0:T(8,128)(2,1)}, bf16[3,2,576,64]{2,3,1,0:T(8,128)(2,1)S(1)}, u32[]{:S(2)}) copy-start(bf16[3,2,576,64]{2,3,1,0:T(8,128)(2,1)S(1)} %get-tuple-element.949) | copy-start | bytes 1327108 | tf_op jit(solution)/shard_map/while
  433.7 11.3 %copy-start.43 = (f32[64]{0:T(128)}, f32[64]{0:T(128)S(1)}, u32[]{:S(2)}) copy-start(f32[64]{0:T(128)S(1)} %get-tuple-element.737) | copy-start | bytes 772 | tf_op jit(solution)/shard_map/while
  433.7 20.9 %copy-start.40 = (f32[64]{0:T(128)}, f32[64]{0:T(128)S(1)}, u32[]{:S(2)}) copy-start(f32[64]{0:T(128)S(1)} %get-tuple-element.752) | copy-start | bytes 772 | tf_op jit(solution)/shard_map/while
  433.7 5.1 copy-start.11
  458.3 4.3 copy-start.12
  513.4 4.6 copy-start.7
  513.4 23.1 %copy-start.5 = (bf16[3,2,576,64]{2,3,1,0:T(8,128)(2,1)}, bf16[3,2,576,64]{2,3,1,0:T(8,128)(2,1)S(1)}, u32[]{:S(2)}) copy-start(bf16[3,2,576,64]{2,3,1,0:T(8,128)(2,1)S(1)} %get-tuple-element.949) | copy-start | bytes 1327108 | tf_op jit(solution)/shard_map/while
  516.0 11.3 %copy-start.43 = (f32[64]{0:T(128)}, f32[64]{0:T(128)S(1)}, u32[]{:S(2)}) copy-start(f32[64]{0:T(128)S(1)} %get-tuple-element.737) | copy-start | bytes 772 | tf_op jit(solution)/shard_map/while
  516.1 20.9 %copy-start.40 = (f32[64]{0:T(128)}, f32[64]{0:T(128)S(1)}, u32[]{:S(2)}) copy-start(f32[64]{0:T(128)S(1)} %get-tuple-element.752) | copy-start | bytes 772 | tf_op jit(solution)/shard_map/while
  516.1 5.1 copy-start.11
  540.6 4.3 copy-start.12
  595.8 4.6 copy-start.7
  595.8 23.1 %copy-start.5 = (bf16[3,2,576,64]{2,3,1,0:T(8,128)(2,1)}, bf16[3,2,576,64]{2,3,1,0:T(8,128)(2,1)S(1)}, u32[]{:S(2)}) copy-start(bf16[3,2,576,64]{2,3,1,0:T(8,128)(2,1)S(1)} %get-tuple-element.949) | copy-start | bytes 1327108 | tf_op jit(solution)/shard_map/while
  598.4 11.3 %copy-start.43 = (f32[64]{0:T(128)}, f32[64]{0:T(128)S(1)}, u32[]{:S(2)}) copy-start(f32[64]{0:T(128)S(1)} %get-tuple-element.737) | copy-start | bytes 772 | tf_op jit(solution)/shard_map/while
  598.4 20.9 %copy-start.40 = (f32[64]{0:T(128)}, f32[64]{0:T(128)S(1)}, u32[]{:S(2)}) copy-start(f32[64]{0:T(128)S(1)} %get-tuple-element.752) | copy-start | bytes 772 | tf_op jit(solution)/shard_map/while
  598.5 5.1 copy-start.11
  (354 other events, 664.6 us)
Sparse Core Ops, SparseCore 0:
  678.3 129.5 all-reduce.53
where the time goes:
time: 827 us; the launch traced here: 817 us
  local copies, waits for them, and re-layouts  424 us (51%)
  other arithmetic  151 us (18%)
  matrix products  85.6 us (10%)
  waiting for transfers between devices  85.1 us (10%)
  blocking collectives  49.3 us (6%)
  between operations  14.1 us (2%)
    concatenate x104, local copies, waits for them, and re-layouts, make_patches(): stacked = jnp.concatenate(taps, axis=3)  192 us
    slice x40, local copies, waits for them, and re-layouts, make_patches(): padded[:, a:a + side, e:e + side, :]  115 us
    psum x1, waiting for transfers between devices, per_device(): summed = lax.psum(conv_grad, ('dp', 'section'))  85.1 us
    while x800, local copies, waits for them, and re-layouts  72.5 us
    convert_element_type x40, other arithmetic, block_forward(): swish(skip + respond(pre_second, gains[1], biases[1], count))  48.6 us
    psum x1, blocking collectives, per_device(): lax.psum((norm_grad, head_w_grad, head_b_grad), ('dp', 'section'))  40.8 us
    convert_element_type x72, other arithmetic, block_forward(): swish(respond(pre_first, gains[0], biases[0], count)).astype(jnp.bfloat16)  37.2 us
    reduce_sum x48, other arithmetic, respond(): return (gain * normed + bias).reshape(values.shape)  36.8 us
  transfers between devices with their start and end apart: 1, of which 1 were waited for; matrix products, arithmetic and copies ran while one was open for 0% of the time, Pallas kernels for 0%

commit v1 on v0

--- a/solution.py
+++ b/solution.py
@@ -147,7 +147,7 @@
     conv_grad, norm_grad, head_w_grad, head_b_grad = accumulate(
         maps, label_groups, all_conv, frn_gain, frn_bias, head_weight, head_bias, total
     )
-    summed = lax.psum(conv_grad, ("dp", "section"))
+    summed = jnp.sum(lax.all_gather(conv_grad, ("dp", "section")), axis=0)
     conv_owned = lax.dynamic_slice_in_dim(summed, offset, share, 3)
     norm_sum, head_w_sum, head_b_sum = lax.psum(
         (norm_grad, head_w_grad, head_b_grad), ("dp", "section")

time: 827 us -> 754 us (0.912)
  local copies, waits for them, and re-layouts: 424 us -> 287 us
  waiting for transfers between devices: 85.1 us -> 141 us
  matrix products: 85.6 us -> 94.8 us
    all_gather x0 -> x1, waiting for transfers between devices: none -> 141 us  [per_device(): summed = jnp.sum(lax.all_gather(conv_grad, ('dp', 'section')), axis=0)]
    psum x1 -> x0, waiting for transfers between devices: 85.1 us -> none  [per_device(): summed = lax.psum(conv_grad, ('dp', 'section'))]
    slice x40, local copies, waits for them, and re-layouts: 115 us -> 54.3 us  [make_patches(): padded[:, a:a + side, e:e + side, :]]
    concatenate x104, local copies, waits for them, and re-layouts: 192 us -> 144 us  [make_patches(): stacked = jnp.concatenate(taps, axis=3)]
    while x800 -> x1216, local copies, waits for them, and re-layouts: 72.5 us -> 43.8 us
    convert_element_type x72, other arithmetic: 37.2 us -> 11.4 us  [block_forward(): swish(respond(pre_first, gains[0], biases[0], count)).astype(jnp.bfloat16)]
    dot_general x24, matrix products: 6.28 us -> 22.4 us  [block_backward(): jnp.dot(cols_second.T, q_second, preferred_element_type=jnp.float32)]
    convert_element_type x40, other arithmetic: 48.6 us -> 33 us  [block_forward(): swish(skip + respond(pre_second, gains[1], biases[1], count))]
where the time goes in v1:
time: 754 us; the launch traced here: 746 us
  local copies, waits for them, and re-layouts  287 us (38%)
  other arithmetic  148 us (20%)
  waiting for transfers between devices  141 us (19%)
  matrix products  94.8 us (13%)
  blocking collectives  50.9 us (7%)
  between operations  14.1 us (2%)
  loops' own time  10.1 us (1%)
    concatenate x104, local copies, waits for them, and re-layouts, make_patches(): stacked = jnp.concatenate(taps, axis=3)  144 us
    all_gather x1, waiting for transfers between devices, per_device(): summed = jnp.sum(lax.all_gather(conv_grad, ('dp', 'section')), axis=0)  141 us
    slice x40, local copies, waits for them, and re-layouts, make_patches(): padded[:, a:a + side, e:e + side, :]  54.3 us
    reduce_sum x48, other arithmetic, respond(): return (gain * normed + bias).reshape(values.shape)  50.5 us
    while x1216, local copies, waits for them, and re-layouts  43.8 us
    psum x1, blocking collectives, per_device(): lax.psum((norm_grad, head_w_grad, head_b_grad), ('dp', 'section'))  42.4 us
    convert_element_type x40, other arithmetic, block_forward(): swish(skip + respond(pre_second, gains[1], biases[1], count))  33 us
    dot_general x24, matrix products, block_backward(): jnp.dot(cols_second.T, q_second, preferred_element_type=jnp.float32)  22.4 us
  transfers between devices with their start and end apart: 1, of which 1 were waited for; matrix products, arithmetic and copies ran while one was open for 0% of the time, Pallas kernels for 0%

profile of v1, /device:TPU:0, one launch (start us, length us, event | category | flops | bytes accessed | tf_op | source)
XLA Modules:
  0.0 745.8 jit_solution(737615511217034903)
XLA Ops:
  7.3 2.1 reshape.932
  9.4 8.5 %all_gather.9 = bf16[3,2,576,64]{2,3,1,0:T(8,128)(2,1)S(1)} all-gather(bf16[3,2,576,16]{2,3,1,0:T(8,128)(2,1)S(1)} %convert_element_type.386), channel_id=1, replica_groups=mesh['dp'=8,'section'=4] {'section'}, dimensions={3}, use_global_device_ids=true | all-gather | bytes 552960 | tf_op jit(solution)/shard_map/all_gather | solution.py:143
  18.6 521.4 %while.19 = (s32[]{:T(128)}, f32[3,2,576,64]{2,3,1,0:T(8,128)}, f32[3,2,2,64]{3,2,1,0:T(2,128)}, f32[64,10]{0,1:T(8,128)}, f32[10]{0:T(128)}, /*index=5*/bf16[8,...) while((s32[]{:T(128)}, f32[3,2,576,64]{2,3,1,0:T(8,128)}, ...), condition=%wide.region_29.30_spmd.clone, body=%wide.region_0.29_spmd.clone.sunk | while | flops 655682368 | bytes 94042408 | solution.py:133
  18.6 1.7 slice_bitcast_fusion.13
  35.2 2.0 concatenate.403
  41.0 2.2 concatenate.404
  43.2 2.1 concatenate.405
  62.9 2.3 multiply_reduce_fusion.38
  66.2 1.6 concatenate.408
  83.7 1.8 slice_bitcast_fusion.13
  100.4 2.0 concatenate.403
  106.1 2.2 concatenate.404
  108.3 2.1 concatenate.405
  128.1 2.3 multiply_reduce_fusion.38
  131.4 1.6 concatenate.408
  148.9 1.8 slice_bitcast_fusion.13
  165.6 2.0 concatenate.403
  171.3 2.2 concatenate.404
  173.5 2.1 concatenate.405
  193.3 2.3 multiply_reduce_fusion.38
  214.1 1.8 slice_bitcast_fusion.13
  230.7 2.0 concatenate.403
  236.5 2.2 concatenate.404
  238.7 2.1 concatenate.405
  258.5 2.3 multiply_reduce_fusion.38
  279.2 1.8 slice_bitcast_fusion.13
  295.9 2.0 concatenate.403
  301.7 2.2 concatenate.404
  303.9 2.1 concatenate.405
  323.6 2.3 multiply_reduce_fusion.38
  344.4 1.8 slice_bitcast_fusion.13
  361.1 2.0 concatenate.403
  366.9 2.2 concatenate.404
  369.0 2.1 concatenate.405
  388.8 2.3 multiply_reduce_fusion.38
  409.6 1.8 slice_bitcast_fusion.13
  426.3 2.0 concatenate.403
  432.0 2.2 concatenate.404
  434.2 2.1 concatenate.405
  454.0 2.3 multiply_reduce_fusion.38
  474.8 1.8 slice_bitcast_fusion.13
  491.4 2.0 concatenate.403
  497.2 2.2 concatenate.404
  499.4 2.1 concatenate.405
  519.2 2.3 multiply_reduce_fusion.38
  540.0 42.4 %all-reduce.51 = (f32[3,2,2,64]{3,2,1,0:T(2,128)S(1)}, f32[64,10]{0,1:T(8,128)S(1)}, f32[10]{0:T(128)S(1)}) all-reduce(f32[3,2,2,64]{3,2,1,0:T(2,128)} %get-tuple-element.962, f32[64,10]{0,1:T(8,128)} %get-tuple-element.963, f32[10]{0:T(128)} %get-tuple-element.964), channel_id=1, replica_groups=mesh['dp'=8,'section'=4] {'dp','section'}, use_global_device_ids=true, to_apply=%region_31.32 | all-reduce | flops 1418 | bytes 11344 | tf_op jit(solution)/shard_map/psum | solution.py:152
  585.5 141.4 %all-gather.3.cloned.1.call-done = f32[96,2,576,64]{2,3,1,0:T(8,128)} async-done(((f32[3,2,576,64]{2,3,1,0:T(8,128)}), f32[96,2,576,64]{2,3,1,0:T(8,128)}) %all-gather.3.cloned.1.call-update) | async-done | bytes 28311568 | tf_op jit(solution)/shard_map/all_gather | solution.py:150
  726.9 11.4 %reduce_sum.441 = f32[3,2,576,64]{2,3,1,0:T(8,128)S(1)} reduce(f32[32,3,2,576,64]{3,4,2,1,0:T(8,128)} %bitcast.784, f32[]{:T(128)} %constant.108.clone.1), dimensions={0}, to_apply=%region_30.31 | reduce | flops 6856704 | bytes 29196292 | tf_op jit(solution)/shard_map/reduce_sum | solution.py:150
  (2066 shorter events, 430.5 us)
Async XLA Ops:
  7.2 10.7 %copy-start.79 = (s32[64]{0:T(128)S(1)}, s32[64]{0:T(128)}, u32[]{:S(2)}) copy-start(s32[64]{0:T(128)} %param.10) | copy-start | bytes 772
  7.2 11.4 %copy-start.47 = (f32[64,10]{0,1:T(8,128)S(1)}, f32[64,10]{0,1:T(8,128)}, u32[]{:S(2)}) copy-start(f32[64,10]{0,1:T(8,128)} %param.14) | copy-start | bytes 7684
  7.2 719.7 %all-gather.3.cloned.1.call-start = ((), (), s32[]{:S(2)}) async-start(), calls=%async_computation | async-start | bytes 32440320 | tf_op jit(solution)/shard_map/all_gather | solution.py:150
  18.6 26.7 %copy-start.3 = (bf16[3,2,576,64]{2,3,1,0:T(8,128)(2,1)}, bf16[3,2,576,64]{2,3,1,0:T(8,128)(2,1)S(1)}, u32[]{:S(2)}) copy-start(bf16[3,2,576,64]{2,3,1,0:T(8,128)(2,1)S(1)} %get-tuple-element.949) | copy-start | bytes 1327108 | tf_op jit(solution)/shard_map/while
  20.3 12.3 %copy-start.51 = (f32[64]{0:T(128)}, f32[64]{0:T(128)S(1)}, u32[]{:S(2)}) copy-start(f32[64]{0:T(128)S(1)} %get-tuple-element.765) | copy-start | bytes 772 | tf_op jit(solution)/shard_map/while
  20.3 18.3 %copy-start.57 = (f32[64]{0:T(128)}, f32[64]{0:T(128)S(1)}, u32[]{:S(2)}) copy-start(f32[64]{0:T(128)S(1)} %get-tuple-element.778) | copy-start | bytes 772 | tf_op jit(solution)/shard_map/while
  20.3 28.8 %copy-start.43 = (f32[64]{0:T(128)}, f32[64]{0:T(128)S(1)}, u32[]{:S(2)}) copy-start(f32[64]{0:T(128)S(1)} %get-tuple-element.799) | copy-start | bytes 772 | tf_op jit(solution)/shard_map/while
  20.3 28.8 %copy-start.45 = (f32[64]{0:T(128)}, f32[64]{0:T(128)S(1)}, u32[]{:S(2)}) copy-start(f32[64]{0:T(128)S(1)} %get-tuple-element.800) | copy-start | bytes 772 | tf_op jit(solution)/shard_map/while
  83.7 26.8 %copy-start.3 = (bf16[3,2,576,64]{2,3,1,0:T(8,128)(2,1)}, bf16[3,2,576,64]{2,3,1,0:T(8,128)(2,1)S(1)}, u32[]{:S(2)}) copy-start(bf16[3,2,576,64]{2,3,1,0:T(8,128)(2,1)S(1)} %get-tuple-element.949) | copy-start | bytes 1327108 | tf_op jit(solution)/shard_map/while
  85.5 12.3 %copy-start.51 = (f32[64]{0:T(128)}, f32[64]{0:T(128)S(1)}, u32[]{:S(2)}) copy-start(f32[64]{0:T(128)S(1)} %get-tuple-element.765) | copy-start | bytes 772 | tf_op jit(solution)/shard_map/while
  85.5 18.3 %copy-start.57 = (f32[64]{0:T(128)}, f32[64]{0:T(128)S(1)}, u32[]{:S(2)}) copy-start(f32[64]{0:T(128)S(1)} %get-tuple-element.778) | copy-start | bytes 772 | tf_op jit(solution)/shard_map/while
  85.5 28.8 %copy-start.43 = (f32[64]{0:T(128)}, f32[64]{0:T(128)S(1)}, u32[]{:S(2)}) copy-start(f32[64]{0:T(128)S(1)} %get-tuple-element.799) | copy-start | bytes 772 | tf_op jit(solution)/shard_map/while
  85.5 28.8 %copy-start.45 = (f32[64]{0:T(128)}, f32[64]{0:T(128)S(1)}, u32[]{:S(2)}) copy-start(f32[64]{0:T(128)S(1)} %get-tuple-element.800) | copy-start | bytes 772 | tf_op jit(solution)/shard_map/while
  148.9 26.8 %copy-start.3 = (bf16[3,2,576,64]{2,3,1,0:T(8,128)(2,1)}, bf16[3,2,576,64]{2,3,1,0:T(8,128)(2,1)S(1)}, u32[]{:S(2)}) copy-start(bf16[3,2,576,64]{2,3,1,0:T(8,128)(2,1)S(1)} %get-tuple-element.949) | copy-start | bytes 1327108 | tf_op jit(solution)/shard_map/while
  150.7 9.0 %copy-start.55 = (f32[64]{0:T(128)}, f32[64]{0:T(128)S(1)}, u32[]{:S(2)}) copy-start(f32[64]{0:T(128)S(1)} %get-tuple-element.752) | copy-start | bytes 772 | tf_op jit(solution)/shard_map/while
  150.7 12.3 %copy-start.51 = (f32[64]{0:T(128)}, f32[64]{0:T(128)S(1)}, u32[]{:S(2)}) copy-start(f32[64]{0:T(128)S(1)} %get-tuple-element.765) | copy-start | bytes 772 | tf_op jit(solution)/shard_map/while
  150.7 18.3 %copy-start.57 = (f32[64]{0:T(128)}, f32[64]{0:T(128)S(1)}, u32[]{:S(2)}) copy-start(f32[64]{0:T(128)S(1)} %get-tuple-element.778) | copy-start | bytes 772 | tf_op jit(solution)/shard_map/while
  150.7 28.8 %copy-start.43 = (f32[64]{0:T(128)}, f32[64]{0:T(128)S(1)}, u32[]{:S(2)}) copy-start(f32[64]{0:T(128)S(1)} %get-tuple-element.799) | copy-start | bytes 772 | tf_op jit(solution)/shard_map/while
  150.7 28.8 %copy-start.45 = (f32[64]{0:T(128)}, f32[64]{0:T(128)S(1)}, u32[]{:S(2)}) copy-start(f32[64]{0:T(128)S(1)} %get-tuple-element.800) | copy-start | bytes 772 | tf_op jit(solution)/shard_map/while
  214.1 26.8 %copy-start.3 = (bf16[3,2,576,64]{2,3,1,0:T(8,128)(2,1)}, bf16[3,2,576,64]{2,3,1,0:T(8,128)(2,1)S(1)}, u32[]{:S(2)}) copy-start(bf16[3,2,576,64]{2,3,1,0:T(8,128)(2,1)S(1)} %get-tuple-element.949) | copy-start | bytes 1327108 | tf_op jit(solution)/shard_map/while
  215.8 9.0 %copy-start.55 = (f32[64]{0:T(128)}, f32[64]{0:T(128)S(1)}, u32[]{:S(2)}) copy-start(f32[64]{0:T(128)S(1)} %get-tuple-element.752) | copy-start | bytes 772 | tf_op jit(solution)/shard_map/while
  215.9 12.3 %copy-start.51 = (f32[64]{0:T(128)}, f32[64]{0:T(128)S(1)}, u32[]{:S(2)}) copy-start(f32[64]{0:T(128)S(1)} %get-tuple-element.765) | copy-start | bytes 772 | tf_op jit(solution)/shard_map/while
  215.9 18.3 %copy-start.57 = (f32[64]{0:T(128)}, f32[64]{0:T(128)S(1)}, u32[]{:S(2)}) copy-start(f32[64]{0:T(128)S(1)} %get-tuple-element.778) | copy-start | bytes 772 | tf_op jit(solution)/shard_map/while
  215.9 28.8 %copy-start.43 = (f32[64]{0:T(128)}, f32[64]{0:T(128)S(1)}, u32[]{:S(2)}) copy-start(f32[64]{0:T(128)S(1)} %get-tuple-element.799) | copy-start | bytes 772 | tf_op jit(solution)/shard_map/while
  215.9 28.8 %copy-start.45 = (f32[64]{0:T(128)}, f32[64]{0:T(128)S(1)}, u32[]{:S(2)}) copy-start(f32[64]{0:T(128)S(1)} %get-tuple-element.800) | copy-start | bytes 772 | tf_op jit(solution)/shard_map/while
  279.2 26.8 %copy-start.3 = (bf16[3,2,576,64]{2,3,1,0:T(8,128)(2,1)}, bf16[3,2,576,64]{2,3,1,0:T(8,128)(2,1)S(1)}, u32[]{:S(2)}) copy-start(bf16[3,2,576,64]{2,3,1,0:T(8,128)(2,1)S(1)} %get-tuple-element.949) | copy-start | bytes 1327108 | tf_op jit(solution)/shard_map/while
  281.0 12.3 %copy-start.51 = (f32[64]{0:T(128)}, f32[64]{0:T(128)S(1)}, u32[]{:S(2)}) copy-start(f32[64]{0:T(128)S(1)} %get-tuple-element.765) | copy-start | bytes 772 | tf_op jit(solution)/shard_map/while
  281.0 18.3 %copy-start.57 = (f32[64]{0:T(128)}, f32[64]{0:T(128)S(1)}, u32[]{:S(2)}) copy-start(f32[64]{0:T(128)S(1)} %get-tuple-element.778) | copy-start | bytes 772 | tf_op jit(solution)/shard_map/while
  281.1 28.8 %copy-start.43 = (f32[64]{0:T(128)}, f32[64]{0:T(128)S(1)}, u32[]{:S(2)}) copy-start(f32[64]{0:T(128)S(1)} %get-tuple-element.799) | copy-start | bytes 772 | tf_op jit(solution)/shard_map/while
  281.1 28.8 %copy-start.45 = (f32[64]{0:T(128)}, f32[64]{0:T(128)S(1)}, u32[]{:S(2)}) copy-start(f32[64]{0:T(128)S(1)} %get-tuple-element.800) | copy-start | bytes 772 | tf_op jit(solution)/shard_map/while
  344.4 26.8 %copy-start.3 = (bf16[3,2,576,64]{2,3,1,0:T(8,128)(2,1)}, bf16[3,2,576,64]{2,3,1,0:T(8,128)(2,1)S(1)}, u32[]{:S(2)}) copy-start(bf16[3,2,576,64]{2,3,1,0:T(8,128)(2,1)S(1)} %get-tuple-element.949) | copy-start | bytes 1327108 | tf_op jit(solution)/shard_map/while
  346.2 9.0 %copy-start.55 = (f32[64]{0:T(128)}, f32[64]{0:T(128)S(1)}, u32[]{:S(2)}) copy-start(f32[64]{0:T(128)S(1)} %get-tuple-element.752) | copy-start | bytes 772 | tf_op jit(solution)/shard_map/while
  346.2 12.3 %copy-start.51 = (f32[64]{0:T(128)}, f32[64]{0:T(128)S(1)}, u32[]{:S(2)}) copy-start(f32[64]{0:T(128)S(1)} %get-tuple-element.765) | copy-start | bytes 772 | tf_op jit(solution)/shard_map/while
  346.2 18.3 %copy-start.57 = (f32[64]{0:T(128)}, f32[64]{0:T(128)S(1)}, u32[]{:S(2)}) copy-start(f32[64]{0:T(128)S(1)} %get-tuple-element.778) | copy-start | bytes 772 | tf_op jit(solution)/shard_map/while
  346.2 28.8 %copy-start.43 = (f32[64]{0:T(128)}, f32[64]{0:T(128)S(1)}, u32[]{:S(2)}) copy-start(f32[64]{0:T(128)S(1)} %get-tuple-element.799) | copy-start | bytes 772 | tf_op jit(solution)/shard_map/while
  346.2 28.8 %copy-start.45 = (f32[64]{0:T(128)}, f32[64]{0:T(128)S(1)}, u32[]{:S(2)}) copy-start(f32[64]{0:T(128)S(1)} %get-tuple-element.800) | copy-start | bytes 772 | tf_op jit(solution)/shard_map/while
  409.6 26.8 %copy-start.3 = (bf16[3,2,576,64]{2,3,1,0:T(8,128)(2,1)}, bf16[3,2,576,64]{2,3,1,0:T(8,128)(2,1)S(1)}, u32[]{:S(2)}) copy-start(bf16[3,2,576,64]{2,3,1,0:T(8,128)(2,1)S(1)} %get-tuple-element.949) | copy-start | bytes 1327108 | tf_op jit(solution)/shard_map/while
  411.4 9.0 %copy-start.55 = (f32[64]{0:T(128)}, f32[64]{0:T(128)S(1)}, u32[]{:S(2)}) copy-start(f32[64]{0:T(128)S(1)} %get-tuple-element.752) | copy-start | bytes 772 | tf_op jit(solution)/shard_map/while
  411.4 12.3 %copy-start.51 = (f32[64]{0:T(128)}, f32[64]{0:T(128)S(1)}, u32[]{:S(2)}) copy-start(f32[64]{0:T(128)S(1)} %get-tuple-element.765) | copy-start | bytes 772 | tf_op jit(solution)/shard_map/while
  411.4 18.3 %copy-start.57 = (f32[64]{0:T(128)}, f32[64]{0:T(128)S(1)}, u32[]{:S(2)}) copy-start(f32[64]{0:T(128)S(1)} %get-tuple-element.778) | copy-start | bytes 772 | tf_op jit(solution)/shard_map/while
  411.4 28.8 %copy-start.43 = (f32[64]{0:T(128)}, f32[64]{0:T(128)S(1)}, u32[]{:S(2)}) copy-start(f32[64]{0:T(128)S(1)} %get-tuple-element.799) | copy-start | bytes 772 | tf_op jit(solution)/shard_map/while
  411.4 28.8 %copy-start.45 = (f32[64]{0:T(128)}, f32[64]{0:T(128)S(1)}, u32[]{:S(2)}) copy-start(f32[64]{0:T(128)S(1)} %get-tuple-element.800) | copy-start | bytes 772 | tf_op jit(solution)/shard_map/while
  474.8 26.8 %copy-start.3 = (bf16[3,2,576,64]{2,3,1,0:T(8,128)(2,1)}, bf16[3,2,576,64]{2,3,1,0:T(8,128)(2,1)S(1)}, u32[]{:S(2)}) copy-start(bf16[3,2,576,64]{2,3,1,0:T(8,128)(2,1)S(1)} %get-tuple-element.949) | copy-start | bytes 1327108 | tf_op jit(solution)/shard_map/while
  476.6 12.3 %copy-start.51 = (f32[64]{0:T(128)}, f32[64]{0:T(128)S(1)}, u32[]{:S(2)}) copy-start(f32[64]{0:T(128)S(1)} %get-tuple-element.765) | copy-start | bytes 772 | tf_op jit(solution)/shard_map/while
  476.6 18.3 %copy-start.57 = (f32[64]{0:T(128)}, f32[64]{0:T(128)S(1)}, u32[]{:S(2)}) copy-start(f32[64]{0:T(128)S(1)} %get-tuple-element.778) | copy-start | bytes 772 | tf_op jit(solution)/shard_map/while
  476.6 28.8 %copy-start.43 = (f32[64]{0:T(128)}, f32[64]{0:T(128)S(1)}, u32[]{:S(2)}) copy-start(f32[64]{0:T(128)S(1)} %get-tuple-element.799) | copy-start | bytes 772 | tf_op jit(solution)/shard_map/while
  476.6 28.8 %copy-start.45 = (f32[64]{0:T(128)}, f32[64]{0:T(128)S(1)}, u32[]{:S(2)}) copy-start(f32[64]{0:T(128)S(1)} %get-tuple-element.800) | copy-start | bytes 772 | tf_op jit(solution)/shard_map/while
  726.9 11.4 %copy-start.26 = (f32[3,2,576,16]{2,3,1,0:T(8,128)S(1)}, f32[3,2,576,16]{2,3,1,0:T(8,128)}, u32[]{:S(2)}) copy-start(f32[3,2,576,16]{2,3,1,0:T(8,128)} %param.11) | copy-start | bytes 663556
  (565 other events, 1085.9 us)
Sparse Core Ops, SparseCore 0:
  540.1 186.7 all-gather.2
